TPU v7x, 32 devices: a whole 2x2x4 slice. The times are simulated.
32 devices in a mesh: dom: 8 (over z, y), feat: 4 (over x, core).
Axes of the slice: x: 2, y: 2, z: 4, core: 2. Of those that a mesh axis runs over, the one named last changes fastest.
Arguments:
- features: bfloat16 [32768, 512], P('dom', 'feat'), may hold values from -6 to 6
- theta: bfloat16 [512, 512], P(None, 'feat'), may hold values from -0.25 to 0.25
- incidence: int32 [3, 4096], P(None, 'dom'), may hold values from 0 to 4095, as said below
- edge_weight: float32 [16384], P('dom'), may hold values from 0.5 to 2
- cotangent: bfloat16 [32768, 512], P('dom', 'feat'), may hold values from -6 to 6
Outputs:
- activation: bfloat16 [32768, 512], P('dom', 'feat')
- grad_features: bfloat16 [32768, 512], P('dom', 'feat')
- grad_theta: float32 [512, 512], P('dom', 'feat')
Inputs may be any that keep to these rules, and one draw needn't show every extreme that they name: `incidence`: in the 64 slots from one vertex owner to one hyperedge owner the live slots (weight over zero) come first, at least one of them; some hyperedge owner receives all 64 slots live from every vertex owner.
All inputs are finite; a program needn't handle non-finite values.
Results may differ from a plain program's by a relative error of at most 0.0073.
Values may be sent and summed in bfloat16 or wider, within the bound.
A program may use at most 64 MiB of HBM per device.

v0:
```python
import jax
import jax.numpy as jnp
from jax import lax
from jax.sharding import PartitionSpec as P


def local(features, theta, incidence, edge_weight, cotangent):
    owners = lax.axis_size("dom")
    nvert = features.shape[0]
    cols = features.shape[1]
    nedge = edge_weight.shape[0]
    vert = incidence[0]
    edge = incidence[1]
    weight = incidence[2]
    weight_f = weight.astype(jnp.float32)
    dvis = lax.rsqrt(1.0 + jax.ops.segment_sum(weight_f, vert, num_segments=nvert))
    slot_scale = weight_f * dvis[vert]
    full_rows = lax.all_gather(features, "feat", axis=1, tiled=True)
    projected = jnp.dot(full_rows, theta, preferred_element_type=jnp.float32).astype(jnp.bfloat16)
    message = (slot_scale[:, None] * projected[vert].astype(jnp.float32)).astype(jnp.bfloat16)
    recv_rows, recv_edge, recv_weight = (
        lax.all_to_all(
            message.reshape(owners, -1, cols), "dom", split_axis=0, concat_axis=0, tiled=True
        ),
        lax.all_to_all(edge.reshape(owners, -1), "dom", split_axis=0, concat_axis=0, tiled=True),
        lax.all_to_all(weight.reshape(owners, -1), "dom", split_axis=0, concat_axis=0, tiled=True),
    )
    recv_edge = recv_edge.reshape(-1)
    degree = 1.0 + jax.ops.segment_sum(
        recv_weight.reshape(-1).astype(jnp.float32), recv_edge, num_segments=nedge
    )
    edge_scale = edge_weight / degree

    def edge_side(rows):
        edge_sum = jax.ops.segment_sum(
            rows.reshape(-1, cols).astype(jnp.float32), recv_edge, num_segments=nedge
        )
        edge_rows = (edge_scale[:, None] * edge_sum).astype(jnp.bfloat16)
        return edge_rows[recv_edge].reshape(owners, -1, cols)

    def vertex_side(back):
        terms = weight_f[:, None] * back.reshape(-1, cols).astype(jnp.float32)
        return dvis[:, None] * jax.ops.segment_sum(terms, vert, num_segments=nvert)

    back = lax.all_to_all(edge_side(recv_rows), "dom", split_axis=0, concat_axis=0, tiled=True)
    summed = vertex_side(back)
    sigma = jax.nn.sigmoid(summed)
    activation = (summed * sigma).astype(jnp.bfloat16)
    slope = sigma * (1.0 + summed * (1.0 - sigma))
    grad_summed = cotangent.astype(jnp.float32) * slope
    grad_message = (slot_scale[:, None] * grad_summed[vert]).astype(jnp.bfloat16)
    grad_recv = lax.all_to_all(
        grad_message.reshape(owners, -1, cols), "dom", split_axis=0, concat_axis=0, tiled=True
    )
    grad_back = lax.all_to_all(edge_side(grad_recv), "dom", split_axis=0, concat_axis=0, tiled=True)
    grad_projected = vertex_side(grad_back).astype(jnp.bfloat16)
    theta_full = lax.all_gather(theta, "feat", axis=1, tiled=True)
    theta_mine = lax.dynamic_slice_in_dim(theta_full, lax.axis_index("feat") * cols, cols, 0)
    grad_total = lax.dot_general(
        lax.all_gather(grad_projected, "feat", axis=1, tiled=True),
        theta_mine,
        (((1,), (1,)), ((), ())),
        preferred_element_type=jnp.float32,
    )
    grad_features = grad_total.astype(jnp.bfloat16)
    share = full_rows.shape[1] // owners
    term = lax.dot_general(
        full_rows, grad_projected, (((0,), (0,)), ((), ())), preferred_element_type=jnp.float32
    )
    total = lax.psum(term, "dom")
    grad_theta = lax.dynamic_slice_in_dim(total, lax.axis_index("dom") * share, share, 0)
    return (activation, grad_features, grad_theta)


def solution(mesh):
    placed = (P("dom", "feat"), P(None, "feat"), P(None, "dom"), P("dom"), P("dom", "feat"))
    return jax.shard_map(
        local,
        mesh=mesh,
        in_specs=placed,
        out_specs=(P("dom", "feat"), P("dom", "feat"), P("dom", "feat")),
        check_vma=False,
    )
```

profile of v0, /device:TPU:0, one launch (start us, length us, event | category | flops | bytes accessed | tf_op | source)
XLA Modules:
  0.0 234.5 jit_solution(12169646869658793668)
XLA Ops:
  7.9 0.8 slice_reduce_fusion.1
  9.4 7.3 %all-to-all-start = ((s32[8,1,64]{2,1,0:T(1,128)}), s32[8,1,64]{2,1,0:T(1,128)S(1)}, u32[]{:S(2)}, u32[]{:S(2)}) async-start(s32[8,1,64]{2,1,0:T(1,128)} %all_to_all.24), calls=%async_computation | async-start | bytes 8192 | tf_op jit(solution)/shard_map/all_to_all | solution.py:25
  17.4 0.7 fusion.19
  18.8 4.3 %all-to-all-done = s32[8,1,64]{2,1,0:T(1,128)S(1)} async-done(((s32[8,1,64]{2,1,0:T(1,128)}), s32[8,1,64]{2,1,0:T(1,128)S(1)}, u32[]{:S(2)}, u32[]{:S(2)}) %all-to-all-start) | async-done | bytes 2080 | tf_op jit(solution)/shard_map/all_to_all | solution.py:25
  23.1 3.3 %all-to-all-start.1 = ((s32[8,1,64]{2,1,0:T(1,128)}), s32[8,1,64]{2,1,0:T(1,128)S(1)}, u32[]{:S(2)}, u32[]{:S(2)}) async-start(s32[8,1,64]{2,1,0:T(1,128)} %all_to_all.26), calls=%async_computation.1 | async-start | bytes 8192 | tf_op jit(solution)/shard_map/all_to_all | solution.py:26
  26.5 3.3 %scatter_custom_fusion = f32[4096]{0:T(1024)S(1)} fusion(s32[512]{0:T(512)S(1)} %bitcast.41, f32[512]{0:T(512)S(1)} %bitcast.36, f32[]{:T(128)} %constant.11.clone.1), kind=kCustom, calls=%fused_computation.40 | custom fusion | flops 512 | bytes 16388 | tf_op jit(solution)/shard_map/scatter-add | solution.py:16
  29.8 3.1 %gather_fusion = f32[512]{0:T(512)S(1)} fusion(f32[4096]{0:T(1024)S(1)} %rsqrt.3, s32[1024]{0:T(1024)S(1)} %pad_clamp_fusion.1), kind=kCustom, calls=%fused_computation | custom fusion | bytes 6144 | tf_op jit(solution)/shard_map/gather | solution.py:17
  34.4 3.3 %scatter_custom_fusion.1 = f32[2048]{0:T(1024)S(1)} fusion(s32[512]{0:T(512)S(1)} %reshape.181, f32[512]{0:T(512)S(1)} %reshape.183, f32[]{:T(128)} %constant.11.clone.1), kind=kCustom, calls=%fused_computation.45 | custom fusion | flops 512 | bytes 8196 | tf_op jit(solution)/shard_map/scatter-add | solution.py:29
  37.7 9.6 %all-gather.3.cloned.1.call-done = bf16[4096,512]{1,0:T(8,128)(2,1)} async-done(((bf16[4096,128]{1,0:T(8,128)(2,1)}), bf16[4096,512]{1,0:T(8,128)(2,1)}) %all-gather.3.cloned.1.call-update) | async-done | bytes 4194320 | tf_op jit(solution)/shard_map/all_gather | solution.py:18
  47.3 3.4 %convolution_convert_fusion.1 = bf16[4096,128]{1,0:T(8,128)(2,1)S(1)} fusion(bf16[4096,512]{1,0:T(8,128)(2,1)} %all-gather.3.cloned.1.call-done, bf16[512,128]{1,0:T(8,128)(2,1)S(1)} %copy-done.2), kind=kOutput, calls=%fused_computation.12 | convolution fusion | flops 537395200 | bytes 5373952 | tf_op jit(solution)/shard_map/dot_general | solution.py:19
  50.8 1.3 gather_fusion.1
  52.1 0.8 fusion.10
  52.9 5.5 %all-to-all-start.2 = ((bf16[8,64,128]{2,1,0:T(8,128)(2,1)}), bf16[8,64,128]{2,1,0:T(8,128)(2,1)S(1)}, u32[]{:S(2)}, u32[]{:S(2)}) async-start(bf16[8,64,128]{2,1,0:T(8,128)(2,1)} %fusion.10), calls=%async_computation.2 | async-start | bytes 262144 | tf_op jit(solution)/shard_map/all_to_all | solution.py:22
  58.5 7.3 %all-to-all-done.2 = bf16[8,64,128]{2,1,0:T(8,128)(2,1)S(1)} async-done(((bf16[8,64,128]{2,1,0:T(8,128)(2,1)}), bf16[8,64,128]{2,1,0:T(8,128)(2,1)S(1)}, u32[]{:S(2)}, u32[]{:S(2)}) %all-to-all-start.2) | async-done | bytes 131104 | tf_op jit(solution)/shard_map/all_to_all | solution.py:22
  65.8 2.5 %scatter_custom_fusion.2 = f32[2048,128]{1,0:T(8,128)S(1)} fusion(s32[512]{0:T(512)S(1)} %reshape.181, f32[]{:T(128)} %constant.12.clone.1, bf16[512,128]{1,0:T(8,128)(2,1)S(1)} %bitcast.28), kind=kCustom, calls=%fused_computation.26 | custom fusion | flops 131072 | bytes 1179652 | tf_op jit(solution)/shard_map/scatter-add | solution.py:35
  68.7 1.3 gather_fusion.2
  70.1 9.9 %all_to_all.38 = bf16[8,64,128]{2,1,0:T(8,128)(2,1)S(1)} all-to-all(bf16[8,64,128]{2,1,0:T(8,128)(2,1)S(1)} %bitcast.33), channel_id=1, replica_groups=mesh['dom'=8,'feat'=4] {'dom'}, dimensions={0} | all-to-all | bytes 262144 | tf_op jit(solution)/shard_map/all_to_all | solution.py:45
  79.9 3.8 %scatter_custom_fusion.3 = f32[4096,128]{1,0:T(8,128)} fusion(s32[512]{0:T(512)S(1)} %bitcast.42, f32[]{:T(128)} %constant.12.clone.1, bf16[512,128]{1,0:T(8,128)(2,1)S(1)} %bitcast.34, f32[512]{0:T(512)S(1)} %bitcast.37), kind=kCustom, calls=%fused_computation.22 | custom fusion | flops 196608 | bytes 2230276 | tf_op jit(solution)/shard_map/scatter-add | solution.py:43
  83.7 3.2 %multiply_multiply_fusion = (f32[4096,128]{1,0:T(8,128)S(1)}, bf16[4096,128]{1,0:T(8,128)(2,1)}) fusion(bf16[4096,128]{1,0:T(8,128)(2,1)S(1)} %copy-done.1, f32[4096,128]{1,0:T(8,128)} %scatter_custom_fusion.3, f32[4096]{0:T(1024)S(1)} %rsqrt.3), kind=kLoop, calls=%fused_computation.14 | loop fusion | flops 6291456 | bytes 6307840 | tf_op jit(solution)/shard_map/mul | solution.py:50
  86.9 1.0 gather_fusion.3
  88.1 9.7 %all_to_all.39 = bf16[8,64,128]{2,1,0:T(8,128)(2,1)S(1)} all-to-all(bf16[8,64,128]{2,1,0:T(8,128)(2,1)S(1)} %multiply_convert_fusion.4), channel_id=1, replica_groups=mesh['dom'=8,'feat'=4] {'dom'}, dimensions={0} | all-to-all | bytes 262144 | tf_op jit(solution)/shard_map/all_to_all | solution.py:52
  97.8 2.5 %scatter_custom_fusion.4 = f32[2048,128]{1,0:T(8,128)S(1)} fusion(s32[512]{0:T(512)S(1)} %reshape.181, f32[]{:T(128)} %constant.12.clone.1, bf16[512,128]{1,0:T(8,128)(2,1)S(1)} %bitcast.30), kind=kCustom, calls=%fused_computation.24 | custom fusion | flops 131072 | bytes 1179652 | tf_op jit(solution)/shard_map/scatter-add | solution.py:35
  100.7 1.3 gather_fusion.4
  102.0 9.7 %all_to_all.40 = bf16[8,64,128]{2,1,0:T(8,128)(2,1)S(1)} all-to-all(bf16[8,64,128]{2,1,0:T(8,128)(2,1)S(1)} %bitcast.31), channel_id=1, replica_groups=mesh['dom'=8,'feat'=4] {'dom'}, dimensions={0} | all-to-all | bytes 262144 | tf_op jit(solution)/shard_map/all_to_all | solution.py:55
  111.7 2.9 %scatter_custom_fusion.5 = f32[4096,128]{1,0:T(8,128)S(1)} fusion(s32[512]{0:T(512)S(1)} %bitcast.43, f32[]{:T(128)} %constant.12.clone.1, bf16[512,128]{1,0:T(8,128)(2,1)S(1)} %bitcast.29, f32[512]{0:T(512)S(1)} %bitcast.38), kind=kCustom, calls=%fused_computation.20 | custom fusion | flops 196608 | bytes 2230276 | tf_op jit(solution)/shard_map/scatter-add | solution.py:43
  114.6 0.7 multiply_convert_fusion
  115.4 4.0 %convolution_bitcast_fusion = f32[512,128]{0,1:T(8,128)} fusion(bf16[4096,128]{1,0:T(8,128)(2,1)S(1)} %multiply_convert_fusion, bf16[4096,512]{1,0:T(8,128)(2,1)} %all-gather.3.cloned.1.call-done), kind=kOutput, calls=%fused_computation.17 | convolution fusion | flops 536870912 | bytes 5505024 | tf_op jit(solution)/shard_map/dot_general | solution.py:67
  120.2 6.5 %all_gather.11 = bf16[512,512]{1,0:T(8,128)(2,1)S(1)} all-gather(bf16[512,128]{1,0:T(8,128)(2,1)S(1)} %copy-done.2), channel_id=1, replica_groups=mesh['dom'=8,'feat'=4] {'feat'}, dimensions={1}, use_global_device_ids=true | all-gather | bytes 655360 | tf_op jit(solution)/shard_map/all_gather | solution.py:57
  126.7 60.2 %all-reduce.2.cloned.1.call-done = f32[512,128]{0,1:T(8,128)} async-done(((f32[512,128]{0,1:T(8,128)}), f32[512,128]{0,1:T(8,128)}) %all-reduce.2.cloned.1.call-update) | async-done | bytes 262160 | tf_op jit(solution)/shard_map/psum | solution.py:70
  187.0 0.9 constant_dynamic-slice_fusion
  188.6 34.9 %all-gather.5.cloned.1.call-done = bf16[4096,512]{1,0:T(8,128)(2,1)} async-done(((bf16[4096,128]{1,0:T(8,128)(2,1)}), bf16[4096,512]{1,0:T(8,128)(2,1)}) %all-gather.5.cloned.1.call-update) | async-done | bytes 4194320 | tf_op jit(solution)/shard_map/all_gather | solution.py:60
  223.5 4.4 %convolution_convert_fusion = bf16[4096,128]{1,0:T(8,128)(2,1)} fusion(bf16[4096,512]{1,0:T(8,128)(2,1)} %all-gather.5.cloned.1.call-done, bf16[512,512]{1,0:T(8,128)(2,1)S(1)} %all_gather.11, s32[]{:T(128)S(6)} %select_n.31), kind=kOutput, calls=%fused_computation.11 | convolution fusion | flops 537395200 | bytes 5373956 | tf_op jit(solution)/shard_map/dot_general | solution.py:59
  (36 shorter events, 6.7 us)
Async XLA Ops:
  7.2 30.6 %copy-start.3 = (f32[2048]{0:T(1024)S(1)}, f32[2048]{0:T(1024)}, u32[]{:S(2)}) copy-start(f32[2048]{0:T(1024)} %param.8) | copy-start | bytes 24580
  7.2 40.2 %copy-start.2 = (bf16[512,128]{1,0:T(8,128)(2,1)S(1)}, bf16[512,128]{1,0:T(8,128)(2,1)}, u32[]{:S(2)}) copy-start(bf16[512,128]{1,0:T(8,128)(2,1)} %param.6) | copy-start | bytes 393220
  7.2 40.1 %all-gather.3.cloned.1.call-start = ((), (), s32[]{:S(2)}) async-start(), calls=%async_computation.6 | async-start | bytes 5242880 | tf_op jit(solution)/shard_map/all_gather | solution.py:18
  9.4 13.7 %all-to-all-start = ((s32[8,1,64]{2,1,0:T(1,128)}), s32[8,1,64]{2,1,0:T(1,128)S(1)}, u32[]{:S(2)}, u32[]{:S(2)}) async-start(s32[8,1,64]{2,1,0:T(1,128)} %all_to_all.24), calls=%async_computation | async-start | bytes 8192 | tf_op jit(solution)/shard_map/all_to_all | solution.py:25
  23.1 11.3 %all-to-all-start.1 = ((s32[8,1,64]{2,1,0:T(1,128)}), s32[8,1,64]{2,1,0:T(1,128)S(1)}, u32[]{:S(2)}, u32[]{:S(2)}) async-start(s32[8,1,64]{2,1,0:T(1,128)} %all_to_all.26), calls=%async_computation.1 | async-start | bytes 8192 | tf_op jit(solution)/shard_map/all_to_all | solution.py:26
  52.9 12.9 %all-to-all-start.2 = ((bf16[8,64,128]{2,1,0:T(8,128)(2,1)}), bf16[8,64,128]{2,1,0:T(8,128)(2,1)S(1)}, u32[]{:S(2)}, u32[]{:S(2)}) async-start(bf16[8,64,128]{2,1,0:T(8,128)(2,1)} %fusion.10), calls=%async_computation.2 | async-start | bytes 262144 | tf_op jit(solution)/shard_map/all_to_all | solution.py:22
  58.4 128.5 %all-reduce.2.cloned.1.call-start = ((), (), s32[]{:S(2)}) async-start(), calls=%async_computation.8 | async-start | bytes 524288 | tf_op jit(solution)/shard_map/psum | solution.py:70
  68.7 15.0 %copy-start.1 = (bf16[4096,128]{1,0:T(8,128)(2,1)S(1)}, bf16[4096,128]{1,0:T(8,128)(2,1)}, u32[]{:S(2)}) copy-start(bf16[4096,128]{1,0:T(8,128)(2,1)} %param.9) | copy-start | bytes 3145732
  115.4 4.1 %copy-start = (bf16[4096,128]{1,0:T(8,128)(2,1)}, bf16[4096,128]{1,0:T(8,128)(2,1)S(1)}, u32[]{:S(2)}) copy-start(bf16[4096,128]{1,0:T(8,128)(2,1)S(1)} %multiply_convert_fusion) | copy-start | bytes 3145732
  119.4 104.1 %all-gather.5.cloned.1.call-start = ((), (), s32[]{:S(2)}) async-start(), calls=%async_computation.7 | async-start | bytes 5242880 | tf_op jit(solution)/shard_map/all_gather | solution.py:60
Sparse Core Ops, SparseCore 0:
  9.6 37.7 all-gather.2
  119.6 67.3 all-reduce.1
  189.2 34.2 all-gather.4
where the time goes:
time: 235 us; the launch traced here: 234 us
  waiting for transfers between devices  118 us (50%)
  blocking collectives  35.9 us (15%)
  other arithmetic  26.6 us (11%)
  starting transfers between devices  16.2 us (7%)
  between operations  14 us (6%)
  local copies, waits for them, and re-layouts  12.1 us (5%)
  matrix products  11.9 us (5%)
    psum x1, waiting for transfers between devices, local(): total = lax.psum(term, 'dom')  60.2 us
    all_gather x1, waiting for transfers between devices, local(): lax.all_gather(grad_projected, 'feat', axis=1, tiled=True)  34.9 us
    all_to_all x1, blocking collectives, local(): lax.all_to_all(edge_side(recv_rows), 'dom', split_axis=0, concat_axis=0,...  9.85 us
    all_to_all x1, blocking collectives, local(): lax.all_to_all(grad_message.reshape(owners, -1, cols), 'dom', split_axis=...  9.74 us
    all_to_all x1, blocking collectives, local(): lax.all_to_all(edge_side(grad_recv), 'dom', split_axis=0, concat_axis=0,...  9.74 us
    all_gather x1, waiting for transfers between devices, local(): full_rows = lax.all_gather(features, 'feat', axis=1, tiled=True)  9.59 us
    all_to_all x1, waiting for transfers between devices, local(): lax.all_to_all(message.reshape(owners, -1, cols), 'dom', split_axis=0, co...  7.34 us
    all_to_all x1, starting transfers between devices, local(): lax.all_to_all(edge.reshape(owners, -1), 'dom', split_axis=0, concat_axis...  7.28 us
  transfers between devices with their start and end apart: 6, of which 5 were waited for; matrix products, arithmetic and copies ran while one was open for 6% of the time, Pallas kernels for 0%

commit v1 on v0

--- a/solution.py
+++ b/solution.py
@@ -67,7 +67,7 @@
     term = lax.dot_general(
         full_rows, grad_projected, (((0,), (0,)), ((), ())), preferred_element_type=jnp.float32
     )
-    total = lax.psum(term, "dom")
+    total = jax.lax.all_gather(term, axis_name="dom").sum(axis=0)
     grad_theta = lax.dynamic_slice_in_dim(total, lax.axis_index("dom") * share, share, 0)
     return (activation, grad_features, grad_theta)
 

time: 235 us -> 213 us (0.906)
  waiting for transfers between devices: 118 us -> 92.7 us
  local copies, waits for them, and re-layouts: 12.1 us -> 14.5 us
    psum x1 -> x0, waiting for transfers between devices: 60.2 us -> none  [local(): total = lax.psum(term, 'dom')]
    all_gather x0 -> x1, waiting for transfers between devices: none -> 39 us  [local(): total = jax.lax.all_gather(term, axis_name='dom').sum(axis=0)]
    all_gather x1, waiting for transfers between devices: 34.9 us -> 31.1 us  [local(): lax.all_gather(grad_projected, 'feat', axis=1, tiled=True)]
    unnamed x9 -> x10, local copies, waits for them, and re-layouts: 0.73 us -> 3.95 us
  transfers between devices with their start and end apart: 6 -> 6, of which waited for: 5 -> 5; matrix products, arithmetic and copies ran while one was open for 6% -> 8% of each run, Pallas kernels for 0% -> 0%
where the time goes in v1:
time: 213 us; the launch traced here: 212 us
  waiting for transfers between devices  92.7 us (44%)
  blocking collectives  35.9 us (17%)
  other arithmetic  27.1 us (13%)
  starting transfers between devices  16.2 us (8%)
  local copies, waits for them, and re-layouts  14.5 us (7%)
  between operations  14 us (7%)
  matrix products  11.9 us (6%)
    all_gather x1, waiting for transfers between devices, local(): total = jax.lax.all_gather(term, axis_name='dom').sum(axis=0)  39 us
    all_gather x1, waiting for transfers between devices, local(): lax.all_gather(grad_projected, 'feat', axis=1, tiled=True)  31.1 us
    all_to_all x1, blocking collectives, local(): lax.all_to_all(edge_side(recv_rows), 'dom', split_axis=0, concat_axis=0,...  9.85 us
    all_to_all x1, blocking collectives, local(): lax.all_to_all(grad_message.reshape(owners, -1, cols), 'dom', split_axis=...  9.74 us
    all_to_all x1, blocking collectives, local(): lax.all_to_all(edge_side(grad_recv), 'dom', split_axis=0, concat_axis=0,...  9.74 us
    all_gather x1, waiting for transfers between devices, local(): full_rows = lax.all_gather(features, 'feat', axis=1, tiled=True)  9.58 us
    all_to_all x1, waiting for transfers between devices, local(): lax.all_to_all(message.reshape(owners, -1, cols), 'dom', split_axis=0, co...  7.34 us
    all_to_all x1, starting transfers between devices, local(): lax.all_to_all(edge.reshape(owners, -1), 'dom', split_axis=0, concat_axis...  7.28 us
  transfers between devices with their start and end apart: 6, of which 5 were waited for; matrix products, arithmetic and copies ran while one was open for 8% of the time, Pallas kernels for 0%

profile of v1, /device:TPU:0, one launch (start us, length us, event | category | flops | bytes accessed | tf_op | source)
XLA Modules:
  0.0 212.3 jit_solution(587673213727598264)
XLA Ops:
  7.9 0.8 slice_reduce_fusion.1
  9.4 7.3 %all-to-all-start = ((s32[8,1,64]{2,1,0:T(1,128)}), s32[8,1,64]{2,1,0:T(1,128)S(1)}, u32[]{:S(2)}, u32[]{:S(2)}) async-start(s32[8,1,64]{2,1,0:T(1,128)} %all_to_all.24), calls=%async_computation | async-start | bytes 8192 | tf_op jit(solution)/shard_map/all_to_all | solution.py:25
  17.4 0.7 fusion.19
  18.8 4.3 %all-to-all-done = s32[8,1,64]{2,1,0:T(1,128)S(1)} async-done(((s32[8,1,64]{2,1,0:T(1,128)}), s32[8,1,64]{2,1,0:T(1,128)S(1)}, u32[]{:S(2)}, u32[]{:S(2)}) %all-to-all-start) | async-done | bytes 2080 | tf_op jit(solution)/shard_map/all_to_all | solution.py:25
  23.1 3.3 %all-to-all-start.1 = ((s32[8,1,64]{2,1,0:T(1,128)}), s32[8,1,64]{2,1,0:T(1,128)S(1)}, u32[]{:S(2)}, u32[]{:S(2)}) async-start(s32[8,1,64]{2,1,0:T(1,128)} %all_to_all.26), calls=%async_computation.1 | async-start | bytes 8192 | tf_op jit(solution)/shard_map/all_to_all | solution.py:26
  26.4 3.3 %scatter_custom_fusion = f32[4096]{0:T(1024)S(1)} fusion(s32[512]{0:T(512)S(1)} %bitcast.47, f32[512]{0:T(512)S(1)} %bitcast.42, f32[]{:T(128)} %constant.11.clone.1), kind=kCustom, calls=%fused_computation.41 | custom fusion | flops 512 | bytes 16388 | tf_op jit(solution)/shard_map/scatter-add | solution.py:16
  29.7 3.1 %gather_fusion = f32[512]{0:T(512)S(1)} fusion(f32[4096]{0:T(1024)S(1)} %rsqrt.3, s32[1024]{0:T(1024)S(1)} %pad_clamp_fusion.1), kind=kCustom, calls=%fused_computation | custom fusion | bytes 6144 | tf_op jit(solution)/shard_map/gather | solution.py:17
  34.5 3.3 %scatter_custom_fusion.1 = f32[2048]{0:T(1024)S(1)} fusion(s32[512]{0:T(512)S(1)} %reshape.181, f32[512]{0:T(512)S(1)} %reshape.183, f32[]{:T(128)} %constant.11.clone.1), kind=kCustom, calls=%fused_computation.46 | custom fusion | flops 512 | bytes 8196 | tf_op jit(solution)/shard_map/scatter-add | solution.py:29
  37.7 9.6 %all-gather.5.cloned.1.call-done = bf16[4096,512]{1,0:T(8,128)(2,1)} async-done(((bf16[4096,128]{1,0:T(8,128)(2,1)}), bf16[4096,512]{1,0:T(8,128)(2,1)}) %all-gather.5.cloned.1.call-update) | async-done | bytes 4194320 | tf_op jit(solution)/shard_map/all_gather | solution.py:18
  47.3 3.4 %convolution_convert_fusion.1 = bf16[4096,128]{1,0:T(8,128)(2,1)S(1)} fusion(bf16[4096,512]{1,0:T(8,128)(2,1)} %all-gather.5.cloned.1.call-done, bf16[512,128]{1,0:T(8,128)(2,1)S(1)} %copy-done.2), kind=kOutput, calls=%fused_computation.12 | convolution fusion | flops 537395200 | bytes 5373952 | tf_op jit(solution)/shard_map/dot_general | solution.py:19
  50.8 1.3 gather_fusion.1
  52.1 0.8 fusion.10
  52.9 5.5 %all-to-all-start.2 = ((bf16[8,64,128]{2,1,0:T(8,128)(2,1)}), bf16[8,64,128]{2,1,0:T(8,128)(2,1)S(1)}, u32[]{:S(2)}, u32[]{:S(2)}) async-start(bf16[8,64,128]{2,1,0:T(8,128)(2,1)} %fusion.10), calls=%async_computation.2 | async-start | bytes 262144 | tf_op jit(solution)/shard_map/all_to_all | solution.py:22
  58.5 7.3 %all-to-all-done.2 = bf16[8,64,128]{2,1,0:T(8,128)(2,1)S(1)} async-done(((bf16[8,64,128]{2,1,0:T(8,128)(2,1)}), bf16[8,64,128]{2,1,0:T(8,128)(2,1)S(1)}, u32[]{:S(2)}, u32[]{:S(2)}) %all-to-all-start.2) | async-done | bytes 131104 | tf_op jit(solution)/shard_map/all_to_all | solution.py:22
  65.8 2.5 %scatter_custom_fusion.2 = f32[2048,128]{1,0:T(8,128)S(1)} fusion(s32[512]{0:T(512)S(1)} %reshape.181, f32[]{:T(128)} %constant.12.clone.1, bf16[512,128]{1,0:T(8,128)(2,1)S(1)} %bitcast.34), kind=kCustom, calls=%fused_computation.27 | custom fusion | flops 131072 | bytes 1179652 | tf_op jit(solution)/shard_map/scatter-add | solution.py:35
  68.7 1.3 gather_fusion.2
  70.1 9.9 %all_to_all.38 = bf16[8,64,128]{2,1,0:T(8,128)(2,1)S(1)} all-to-all(bf16[8,64,128]{2,1,0:T(8,128)(2,1)S(1)} %bitcast.39), channel_id=1, replica_groups=mesh['dom'=8,'feat'=4] {'dom'}, dimensions={0} | all-to-all | bytes 262144 | tf_op jit(solution)/shard_map/all_to_all | solution.py:45
  79.9 3.8 %scatter_custom_fusion.3 = f32[4096,128]{1,0:T(8,128)} fusion(s32[512]{0:T(512)S(1)} %bitcast.48, f32[]{:T(128)} %constant.12.clone.1, bf16[512,128]{1,0:T(8,128)(2,1)S(1)} %bitcast.40, f32[512]{0:T(512)S(1)} %bitcast.43), kind=kCustom, calls=%fused_computation.23 | custom fusion | flops 196608 | bytes 2230276 | tf_op jit(solution)/shard_map/scatter-add | solution.py:43
  83.7 3.1 %multiply_multiply_fusion = (f32[4096,128]{1,0:T(8,128)S(1)}, bf16[4096,128]{1,0:T(8,128)(2,1)}) fusion(bf16[4096,128]{1,0:T(8,128)(2,1)S(1)} %copy-done.1, f32[4096,128]{1,0:T(8,128)} %scatter_custom_fusion.3, f32[4096]{0:T(1024)S(1)} %rsqrt.3), kind=kLoop, calls=%fused_computation.15 | loop fusion | flops 6291456 | bytes 6307840 | tf_op jit(solution)/shard_map/mul | solution.py:50
  86.9 1.0 gather_fusion.3
  88.0 9.7 %all_to_all.39 = bf16[8,64,128]{2,1,0:T(8,128)(2,1)S(1)} all-to-all(bf16[8,64,128]{2,1,0:T(8,128)(2,1)S(1)} %multiply_convert_fusion.4), channel_id=1, replica_groups=mesh['dom'=8,'feat'=4] {'dom'}, dimensions={0} | all-to-all | bytes 262144 | tf_op jit(solution)/shard_map/all_to_all | solution.py:52
  97.8 2.5 %scatter_custom_fusion.4 = f32[2048,128]{1,0:T(8,128)S(1)} fusion(s32[512]{0:T(512)S(1)} %reshape.181, f32[]{:T(128)} %constant.12.clone.1, bf16[512,128]{1,0:T(8,128)(2,1)S(1)} %bitcast.36), kind=kCustom, calls=%fused_computation.25 | custom fusion | flops 131072 | bytes 1179652 | tf_op jit(solution)/shard_map/scatter-add | solution.py:35
  100.6 1.3 gather_fusion.4
  102.0 9.7 %all_to_all.40 = bf16[8,64,128]{2,1,0:T(8,128)(2,1)S(1)} all-to-all(bf16[8,64,128]{2,1,0:T(8,128)(2,1)S(1)} %bitcast.37), channel_id=1, replica_groups=mesh['dom'=8,'feat'=4] {'dom'}, dimensions={0} | all-to-all | bytes 262144 | tf_op jit(solution)/shard_map/all_to_all | solution.py:55
  111.7 2.9 %scatter_custom_fusion.5 = f32[4096,128]{1,0:T(8,128)S(1)} fusion(s32[512]{0:T(512)S(1)} %bitcast.49, f32[]{:T(128)} %constant.12.clone.1, bf16[512,128]{1,0:T(8,128)(2,1)S(1)} %bitcast.35, f32[512]{0:T(512)S(1)} %bitcast.44), kind=kCustom, calls=%fused_computation.21 | custom fusion | flops 196608 | bytes 2230276 | tf_op jit(solution)/shard_map/scatter-add | solution.py:43
  114.6 0.7 multiply_convert_fusion
  115.3 4.0 %convolution_bitcast_fusion = f32[512,128]{0,1:T(8,128)} fusion(bf16[4096,128]{1,0:T(8,128)(2,1)S(1)} %multiply_convert_fusion, bf16[4096,512]{1,0:T(8,128)(2,1)} %all-gather.5.cloned.1.call-done), kind=kOutput, calls=%fused_computation.18 | convolution fusion | flops 536870912 | bytes 5505024 | tf_op jit(solution)/shard_map/dot_general | solution.py:67
  120.1 6.5 %all_gather.17 = bf16[512,512]{1,0:T(8,128)(2,1)S(1)} all-gather(bf16[512,128]{1,0:T(8,128)(2,1)S(1)} %copy-done.2), channel_id=1, replica_groups=mesh['dom'=8,'feat'=4] {'feat'}, dimensions={1}, use_global_device_ids=true | all-gather | bytes 655360 | tf_op jit(solution)/shard_map/all_gather | solution.py:57
  126.7 39.0 %all-gather.9.cloned.1.call-done = f32[4096,128]{0,1:T(8,128)} async-done(((f32[512,128]{0,1:T(8,128)}), f32[4096,128]{0,1:T(8,128)}) %all-gather.9.cloned.1.call-update) | async-done | bytes 2097168 | tf_op jit(solution)/shard_map/all_gather | solution.py:70
  165.7 3.2 %copy.9 = f32[16,8,8,512]{3,2,1,0:T(8,128)S(1)} copy(f32[16,8,8,512]{3,1,2,0:T(8,128)} %bitcast.32) | data formatting | bytes 4194304
  170.2 31.1 %all-gather.7.cloned.1.call-done = bf16[4096,512]{1,0:T(8,128)(2,1)} async-done(((bf16[4096,128]{1,0:T(8,128)(2,1)}), bf16[4096,512]{1,0:T(8,128)(2,1)}) %all-gather.7.cloned.1.call-update) | async-done | bytes 4194320 | tf_op jit(solution)/shard_map/all_gather | solution.py:60
  201.3 4.4 %convolution_convert_fusion = bf16[4096,128]{1,0:T(8,128)(2,1)} fusion(bf16[4096,512]{1,0:T(8,128)(2,1)} %all-gather.7.cloned.1.call-done, bf16[512,512]{1,0:T(8,128)(2,1)S(1)} %all_gather.17, s32[]{:T(128)S(6)} %select_n.31), kind=kOutput, calls=%fused_computation.11 | convolution fusion | flops 537395200 | bytes 5373956 | tf_op jit(solution)/shard_map/dot_general | solution.py:59
  (38 shorter events, 7.3 us)
Async XLA Ops:
  7.2 30.6 %copy-start.3 = (f32[2048]{0:T(1024)S(1)}, f32[2048]{0:T(1024)}, u32[]{:S(2)}) copy-start(f32[2048]{0:T(1024)} %param.8) | copy-start | bytes 24580
  7.2 40.2 %copy-start.2 = (bf16[512,128]{1,0:T(8,128)(2,1)S(1)}, bf16[512,128]{1,0:T(8,128)(2,1)}, u32[]{:S(2)}) copy-start(bf16[512,128]{1,0:T(8,128)(2,1)} %param.6) | copy-start | bytes 393220
  7.2 40.1 %all-gather.5.cloned.1.call-start = ((), (), s32[]{:S(2)}) async-start(), calls=%async_computation.6 | async-start | bytes 5242880 | tf_op jit(solution)/shard_map/all_gather | solution.py:18
  9.4 13.7 %all-to-all-start = ((s32[8,1,64]{2,1,0:T(1,128)}), s32[8,1,64]{2,1,0:T(1,128)S(1)}, u32[]{:S(2)}, u32[]{:S(2)}) async-start(s32[8,1,64]{2,1,0:T(1,128)} %all_to_all.24), calls=%async_computation | async-start | bytes 8192 | tf_op jit(solution)/shard_map/all_to_all | solution.py:25
  23.1 11.2 %all-to-all-start.1 = ((s32[8,1,64]{2,1,0:T(1,128)}), s32[8,1,64]{2,1,0:T(1,128)S(1)}, u32[]{:S(2)}, u32[]{:S(2)}) async-start(s32[8,1,64]{2,1,0:T(1,128)} %all_to_all.26), calls=%async_computation.1 | async-start | bytes 8192 | tf_op jit(solution)/shard_map/all_to_all | solution.py:26
  52.9 12.9 %all-to-all-start.2 = ((bf16[8,64,128]{2,1,0:T(8,128)(2,1)}), bf16[8,64,128]{2,1,0:T(8,128)(2,1)S(1)}, u32[]{:S(2)}, u32[]{:S(2)}) async-start(bf16[8,64,128]{2,1,0:T(8,128)(2,1)} %fusion.10), calls=%async_computation.2 | async-start | bytes 262144 | tf_op jit(solution)/shard_map/all_to_all | solution.py:22
  58.4 107.2 %all-gather.9.cloned.1.call-start = ((), (), s32[]{:S(2)}) async-start(), calls=%async_computation.8 | async-start | bytes 2359296 | tf_op jit(solution)/shard_map/all_gather | solution.py:70
  68.7 15.0 %copy-start.1 = (bf16[4096,128]{1,0:T(8,128)(2,1)S(1)}, bf16[4096,128]{1,0:T(8,128)(2,1)}, u32[]{:S(2)}) copy-start(bf16[4096,128]{1,0:T(8,128)(2,1)} %param.9) | copy-start | bytes 3145732
  115.3 4.0 %copy-start = (bf16[4096,128]{1,0:T(8,128)(2,1)}, bf16[4096,128]{1,0:T(8,128)(2,1)S(1)}, u32[]{:S(2)}) copy-start(bf16[4096,128]{1,0:T(8,128)(2,1)S(1)} %multiply_convert_fusion) | copy-start | bytes 3145732
  119.4 81.9 %all-gather.7.cloned.1.call-start = ((), (), s32[]{:S(2)}) async-start(), calls=%async_computation.7 | async-start | bytes 5242880 | tf_op jit(solution)/shard_map/all_gather | solution.py:60
Sparse Core Ops, SparseCore 0:
  9.6 37.7 all-gather.4
  119.5 46.0 all-gather.8
  167.8 33.4 all-gather.6
